TPU v7x, 128 devices: a whole 4x4x4 slice. The times are simulated.
128 devices in a mesh: row: 16 (over x, z), col: 8 (over y, core).
Axes of the slice: x: 4, y: 4, z: 4, core: 2. Of those that a mesh axis runs over, the one named last changes fastest.
Arguments:
- far_left: bfloat16 [16, 8, 128, 128, 256], P('row', 'col'), may hold values from -6.92749e-05 to 6.92749e-05
- far_right: bfloat16 [16, 8, 128, 128, 256], P('row', 'col'), may hold values from -0.47 to 0.47
- far_rank: int32 [16, 8, 128], P('row', 'col'), may hold values from 8 to 128, as said below
- near_tiles: bfloat16 [128, 3, 256, 256], P(('row', 'col')), may hold values from -0.0004108677 to 0.0004108677
- near_cols: int32 [128, 3], P(('row', 'col')), may hold values from 0 to 15, as said below
- data: float32 [16, 8, 256, 128], P('row', 'col'), may hold values from -40 to 40
- reg_weight: float32 [128], replicated, may hold values from 0.05 to 0.5
Outputs:
- solution: float32 [8, 16, 256, 128], P('col', 'row')
- misfit: float32 [16, 8, 256, 128], P('row', 'col')
- regularized: float32 [8, 16, 256, 128], P('col', 'row')
Inputs may be any that keep to these rules, and one draw needn't show every extreme that they name: `far_rank`: each leaf's rank is 128 divided by a power of two, at least 1; the first leaf of every device block has rank 128. `near_cols`: the 3 columns of a leaf row I are distinct and lie among five neighbouring leaf columns that contain I % 16 or touch the edge of the column block.
All inputs are finite; a program needn't handle non-finite values.
Results may differ from a plain program's by a relative error of at most 0.0085.
Values may be sent and summed in bfloat16 or wider, within the bound.
No kernel may reach another device: no remote copies, remote signals or barrier semaphores. Data moves between devices by JAX's collectives and lax.ppermute only.
A program may use at most 128 MiB of HBM per device.

v0:
```python
import jax
import jax.numpy as jnp
from jax import lax
from jax.sharding import PartitionSpec as P

LEAF_ROWS = 8
ITERS = 2


def padded_2(cells, sides, width, closed):
    for axis, dim in sides:
        count = lax.axis_size(axis)
        ends = count if closed else count - 1
        head = lax.slice_in_dim(cells, 0, width, axis=dim)
        tail = lax.slice_in_dim(cells, cells.shape[dim] - width, cells.shape[dim], axis=dim)
        cells = jnp.concatenate(
            [
                lax.ppermute(tail, axis, [(i, (i + 1) % count) for i in range(ends)]),
                cells,
                lax.ppermute(head, axis, [((i + 1) % count, i) for i in range(ends)]),
            ],
            axis=dim,
        )
    return cells


def column_sums(values):
    return jnp.sum(values, axis=0)


def per_device(far_left, far_right, far_rank, near_tiles, near_cols, data, reg_weight):
    row_count = lax.axis_size("row")
    col_count = lax.axis_size("col")
    row_ratio = row_count // col_count
    row_at = lax.axis_index("row")
    col_at = lax.axis_index("col")
    leaf_size = far_left.shape[-1]
    rank_max = far_left.shape[-2]
    rows_leaf = LEAF_ROWS
    cols_leaf = rows_leaf * row_ratio
    piece_rows = data.shape[2]
    experiments = data.shape[3]
    left_factor = far_left.reshape(rows_leaf, cols_leaf, rank_max, leaf_size)
    right_factor = far_right.reshape(rows_leaf, cols_leaf, rank_max, leaf_size)
    live_slots = lax.broadcasted_iota(
        jnp.int32, (rows_leaf * cols_leaf, rank_max), 1
    ) < far_rank.reshape(-1, 1)
    rank_mask = live_slots.astype(jnp.float32).reshape(rows_leaf, cols_leaf, rank_max, 1)
    is_owner = col_at == row_at // row_ratio
    tiles_all, cols_all = (
        lax.all_gather(near_tiles, "col", axis=0, tiled=True),
        lax.all_gather(near_cols, "col", axis=0, tiled=True),
    )

    def place_columns(term_list, columns, col_limit):
        flattened = term_list.reshape(-1, leaf_size, experiments)
        onehot = (columns.reshape(-1, 1) == jnp.arange(col_limit, dtype=jnp.int32)[None, :]).astype(
            jnp.float32
        )
        return jnp.einsum(
            "ec,eqn->cqn",
            onehot,
            flattened,
            precision=lax.Precision.HIGHEST,
            preferred_element_type=jnp.float32,
        )

    def adjoint(block_in):
        coefficient = jnp.einsum(
            "ijkp,ipn->ijkn", left_factor, block_in, preferred_element_type=jnp.float32
        )
        coefficient = (coefficient * rank_mask).astype(jnp.bfloat16)
        partial_value = jnp.einsum(
            "ijkq,ijkn->jqn", right_factor, coefficient, preferred_element_type=jnp.float32
        )

        def adjoint_near_part():
            term_list = jnp.einsum(
                "ibpq,ipn->ibqn", tiles_all, block_in, preferred_element_type=jnp.float32
            )
            return place_columns(term_list, cols_all, cols_leaf)

        partial_value = partial_value + lax.cond(
            is_owner, adjoint_near_part, lambda: jnp.zeros_like(partial_value)
        )
        return partial_value

    def apply_transpose(vector):
        gathered = lax.all_gather(vector.astype(jnp.bfloat16), "col", axis=0, tiled=True)
        partial_value = adjoint(gathered.reshape(rows_leaf, leaf_size, experiments))
        return lax.psum_scatter(
            partial_value.reshape(-1, experiments), "row", scatter_dimension=0, tiled=True
        )

    def smoothing(vector):
        padded = padded_2(vector.astype(jnp.bfloat16), (("row", 0),), 1, True).astype(vector.dtype)
        rim_pair = jnp.stack([padded[-1], padded[0]])
        outer_rims = padded_2(rim_pair, (("col", 0),), 1, False)
        lower_rim = jnp.where(row_at == 0, outer_rims[0], padded[0])
        upper_rim = jnp.where(row_at == row_count - 1, outer_rims[3], padded[-1])
        shift_below = jnp.concatenate([lower_rim[None], vector[:-1]], axis=0)
        shift_above = jnp.concatenate([vector[1:], upper_rim[None]], axis=0)
        return 2.0 * vector - shift_below - shift_above

    residual = data.reshape(piece_rows, experiments)
    solution = jnp.zeros((piece_rows, experiments), jnp.float32)
    descent = apply_transpose(residual)
    direction = descent

    def gradient_total(vector):
        return lax.psum(column_sums(vector * vector), ("row", "col"))

    gradient_sq = gradient_total(descent)
    for iteration in range(ITERS):
        apply_gathered = lax.all_gather(direction.astype(jnp.bfloat16), "row", axis=0, tiled=True)
        forward_block_in = apply_gathered.reshape(cols_leaf, leaf_size, experiments)
        forward_coefficient = jnp.einsum(
            "ijkq,jqn->ijkn", right_factor, forward_block_in, preferred_element_type=jnp.float32
        )
        forward_coefficient = (forward_coefficient * rank_mask).astype(jnp.bfloat16)
        forward_partial_value = jnp.einsum(
            "ijkp,ijkn->ipn", left_factor, forward_coefficient, preferred_element_type=jnp.float32
        )

        def forward_near_part():
            chosen = forward_block_in[cols_all]
            return jnp.einsum(
                "ibpq,ibqn->ipn", tiles_all, chosen, preferred_element_type=jnp.float32
            )

        forward_partial_value = forward_partial_value + lax.cond(
            is_owner, forward_near_part, lambda: jnp.zeros_like(forward_partial_value)
        )
        mapped = lax.psum_scatter(
            forward_partial_value.reshape(-1, experiments).astype(jnp.bfloat16),
            "col",
            scatter_dimension=0,
            tiled=True,
        ).astype(jnp.float32)
        curved = smoothing(direction)
        pair_sums = jnp.stack([column_sums(mapped * mapped), column_sums(direction * curved)])
        totals = lax.psum(pair_sums, ("row", "col"))
        step_size = gradient_sq / (totals[0] + reg_weight * totals[1])
        solution = solution + step_size * direction
        residual = residual - step_size * mapped
        if iteration + 1 < ITERS:
            descent = apply_transpose(residual) - reg_weight * smoothing(solution)
            fresh_norm = gradient_total(descent)
            direction = descent + fresh_norm / gradient_sq * direction
            gradient_sq = fresh_norm
    penalty_image = smoothing(solution)
    solution_out = solution.reshape(1, 1, piece_rows, experiments)
    misfit_out = residual.reshape(1, 1, piece_rows, experiments)
    penalty_out = penalty_image.reshape(1, 1, piece_rows, experiments)
    return (solution_out, misfit_out, penalty_out)


def solution(mesh):
    in_specs = (
        P("row", "col", None, None, None),
        P("row", "col", None, None, None),
        P("row", "col", None),
        P(("row", "col"), None, None, None),
        P(("row", "col"), None),
        P("row", "col", None, None),
        P(),
    )
    out_specs = (
        P("col", "row", None, None),
        P("row", "col", None, None),
        P("col", "row", None, None),
    )
    return jax.shard_map(
        per_device, mesh=mesh, in_specs=in_specs, out_specs=out_specs, check_vma=False
    )
```

profile of v0, /device:TPU:0, one launch (start us, length us, event | category | flops | bytes accessed | tf_op | source)
XLA Modules:
  0.0 655.7 jit_solution(8412940083033084894)
XLA Ops:
  7.9 11.0 %all-gather = s32[8,1,3]{2,1,0:T(1,128)S(1)} all-gather(s32[1,1,3]{2,1,0:T(1,128)} %bitcast.185), channel_id=1, replica_groups=mesh['row'=16,'col'=8] {'col'}, dimensions={0}, use_global_device_ids=true | all-gather | bytes 108 | tf_op jit(solution)/shard_map/all_gather | solution.py:52
  22.0 15.0 %all_gather.18 = bf16[2048,128]{1,0:T(8,128)(2,1)} all-gather(bf16[256,128]{1,0:T(8,128)(2,1)S(1)} %bitcast_convert_fusion), channel_id=1, replica_groups=mesh['row'=16,'col'=8] {'col'}, dimensions={0}, use_global_device_ids=true | all-gather | bytes 589824 | tf_op jit(solution)/shard_map/all_gather | solution.py:89
  37.0 5.1 all-gather.5.cloned.1.call-done
  42.1 10.6 %conditional.4 = (f32[16,256,128]{1,2,0:T(8,128)}) conditional(s32[]{:T(128)} %convert_element_type.83, () %tuple.32, (s32[8,3]{0,1:T(4,128)S(1)}, bf16[8,3,256,256]{3,2,1,0:T(8,128)(2,1)}, bf16[8,256,128]{2,1,0:T(8,128)(2,1)}) %tuple.108), branch_computations={%region_0.1_spmd, %region_1.2_spmd} | conditional | flops 553648512 | bytes 16253416 | solution.py:83
  52.7 9.6 %bitcast_add_fusion.1 = f32[16,256,128]{1,2,0:T(8,128)} fusion(f32[16,256,128]{1,2,0:T(8,128)} %get-tuple-element.99, bf16[8,16,128,256]{3,2,1,0:T(8,128)(2,1)} %bitcast.154, f32[8,16,128]{2,1,0:T(8,128)S(1)} %fusion.82, bf16[8,16,128,256]{3,2,1,0:T(8,128)(2,1)} %bitcast.158, bf16[8,256,128,1]{2,1,3,0:T(8,128)(2,1)} %bitcast.176), kind=kOutput, calls=%fused_computation.42 | convolution fusion | flops 2152202240 | bytes 21561344 | tf_op jit(solution)/shard_map/ijkq,ijkn->jqn/dot_general | solution.py:73
  65.4 74.4 %reduce-scatter.5.cloned.1.call-done = f32[256,128]{1,0:T(8,128)} async-done(((f32[4096,128]{1,0:T(8,128)}), f32[256,128]{1,0:T(8,128)}) %reduce-scatter.5.cloned.1.call-update) | async-done | bytes 131088 | tf_op jit(solution)/shard_map/reduce_scatter | solution.py:91
  141.4 43.3 %all-gather.7.cloned.1.call-done = bf16[4096,128]{1,0:T(8,128)(2,1)} async-done(((bf16[256,128]{1,0:T(8,128)(2,1)}), bf16[4096,128]{1,0:T(8,128)(2,1)}) %all-gather.7.cloned.1.call-update) | async-done | bytes 1048592 | tf_op jit(solution)/shard_map/all_gather | solution.py:115
  184.7 7.0 %conditional.5 = (f32[8,256,128]{1,2,0:T(8,128)}) conditional(s32[]{:T(128)} %convert_element_type.83, () %tuple.34, (s32[8,3]{0,1:T(4,128)S(1)}, bf16[16,256,128]{2,1,0:T(8,128)(2,1)}, bf16[8,3,256,256]{3,2,1,0:T(8,128)(2,1)S(1)}) %tuple.109), branch_computations={%region_5.6_spmd, %region_6.7_spmd} | conditional | flops 402654272 | bytes 8917768 | solution.py:131
  191.7 10.0 %fusion.62 = bf16[8,256,128]{1,2,0:T(8,128)(2,1)} fusion(f32[8,256,128]{1,2,0:T(8,128)} %get-tuple-element.143, bf16[8,16,128,256]{3,2,1,0:T(8,128)(2,1)} %bitcast.159, f32[8,16,128]{2,1,0:T(8,128)S(1)} %fusion.82, bf16[16,256,128,1]{2,1,0,3:T(8,128)(2,1)} %bitcast.165, bf16[8,16,128,256]{3,2,1,0:T(8,128)(2,1)} %bitcast.155), kind=kOutput, calls=%fused_computation.50 | convolution fusion | flops 2152202240 | bytes 19464192 | tf_op jit(solution)/shard_map/ijkp,ijkn->ipn/dot_general | solution.py:121
  216.6 16.3 %reduce-scatter.7.cloned.1.call-done = bf16[256,128]{1,0:T(8,128)(2,1)} async-done(((bf16[2048,128]{1,0:T(8,128)(2,1)}), bf16[256,128]{1,0:T(8,128)(2,1)}) %reduce-scatter.7.cloned.1.call-update) | async-done | bytes 65552 | tf_op jit(solution)/shard_map/reduce_scatter | solution.py:134
  233.7 65.1 %all-reduce = (f32[128]{0:T(128)S(1)}, f32[2,128]{1,0:T(2,128)S(1)}) all-reduce(f32[128]{0:T(128)S(1)} %get-tuple-element.102, f32[2,128]{1,0:T(2,128)S(1)} %pad_maximum_fusion), channel_id=1, replica_groups=mesh['row'=16,'col'=8] {'row','col'}, use_global_device_ids=true, to_apply=%region_4.5 | all-reduce | flops 384 | bytes 3072 | tf_op jit(solution)/shard_map/psum | solution.py:111
  300.9 14.2 %all_gather.22 = bf16[2048,128]{1,0:T(8,128)(2,1)} all-gather(bf16[256,128]{1,0:T(8,128)(2,1)S(1)} %get-tuple-element.138), channel_id=1, replica_groups=mesh['row'=16,'col'=8] {'col'}, dimensions={0}, use_global_device_ids=true | all-gather | bytes 589824 | tf_op jit(solution)/shard_map/all_gather | solution.py:89
  315.1 13.1 %conditional.6 = (f32[16,256,128]{1,2,0:T(8,128)}) conditional(s32[]{:T(128)} %convert_element_type.83, () %tuple.36, (s32[8,3]{0,1:T(4,128)S(1)}, bf16[8,3,256,256]{3,2,1,0:T(8,128)(2,1)S(1)}, bf16[8,256,128]{2,1,0:T(8,128)(2,1)}) %tuple.110), branch_computations={%region_11.12_spmd, %region_12.13_spmd} | conditional | flops 553648512 | bytes 16253416 | solution.py:83
  319.1 6.2 fusion.7
  328.2 11.9 %bitcast_add_fusion = f32[16,256,128]{1,2,0:T(8,128)} fusion(f32[16,256,128]{1,2,0:T(8,128)} %get-tuple-element.100, bf16[8,16,128,256]{3,2,1,0:T(8,128)(2,1)} %bitcast.156, f32[8,16,128]{2,0,1:T(8,128)S(1)} %copy-done.11, bf16[8,256,128,1]{2,1,0,3:T(8,128)(2,1)} %bitcast.39, bf16[8,16,128,256]{3,2,1,0:T(8,128)(2,1)} %bitcast.160), kind=kOutput, calls=%fused_computation.41 | convolution fusion | flops 2152202240 | bytes 21561344 | tf_op jit(solution)/shard_map/ijkq,ijkn->jqn/dot_general | solution.py:73
  343.3 5.2 collective-permute-start.5
  355.5 58.6 %reduce-scatter.9.cloned.1.call-done = f32[256,128]{1,0:T(8,128)} async-done(((f32[4096,128]{1,0:T(8,128)}), f32[256,128]{1,0:T(8,128)}) %reduce-scatter.9.cloned.1.call-update) | async-done | bytes 131088 | tf_op jit(solution)/shard_map/reduce_scatter | solution.py:91
  416.3 64.6 %psum.30 = f32[128]{0:T(128)S(1)} all-reduce(f32[128]{0:T(128)} %get-tuple-element.109), channel_id=1, replica_groups=mesh['row'=16,'col'=8] {'row','col'}, use_global_device_ids=true, to_apply=%region_15.16 | all-reduce | flops 128 | bytes 1024 | tf_op jit(solution)/shard_map/psum | solution.py:111
  483.1 39.0 %all-gather.9.cloned.1.call-done = bf16[4096,128]{1,0:T(8,128)(2,1)} async-done(((bf16[256,128]{1,0:T(8,128)(2,1)}), bf16[4096,128]{1,0:T(8,128)(2,1)}) %all-gather.9.cloned.1.call-update) | async-done | bytes 1048592 | tf_op jit(solution)/shard_map/all_gather | solution.py:115
  522.1 6.9 %conditional.7 = (f32[8,256,128]{1,2,0:T(8,128)}) conditional(s32[]{:T(128)} %convert_element_type.83, () %tuple.38, (s32[8,3]{0,1:T(4,128)S(1)}, bf16[16,256,128]{2,1,0:T(8,128)(2,1)}, bf16[8,3,256,256]{3,2,1,0:T(8,128)(2,1)S(1)}) %tuple.111), branch_computations={%region_16.17_spmd, %region_17.18_spmd} | conditional | flops 402654272 | bytes 8917768 | solution.py:131
  529.1 9.3 %fusion.59 = bf16[8,256,128]{1,2,0:T(8,128)(2,1)S(1)} fusion(f32[8,256,128]{1,2,0:T(8,128)} %get-tuple-element.144, bf16[8,16,128,256]{3,2,1,0:T(8,128)(2,1)} %bitcast.161, f32[8,16,128]{2,1,0:T(8,128)S(1)} %copy-done.6, bf16[16,256,128,1]{2,1,0,3:T(8,128)(2,1)} %bitcast.163, bf16[8,16,128,256]{3,2,1,0:T(8,128)(2,1)} %bitcast.157), kind=kOutput, calls=%fused_computation.49 | convolution fusion | flops 2152202240 | bytes 19464192 | tf_op jit(solution)/shard_map/ijkp,ijkn->ipn/dot_general | solution.py:121
  551.6 17.0 %reduce-scatter.11.cloned.1.call-done = bf16[256,128]{1,0:T(8,128)(2,1)} async-done(((bf16[2048,128]{1,0:T(8,128)(2,1)}), bf16[256,128]{1,0:T(8,128)(2,1)}) %reduce-scatter.11.cloned.1.call-update) | async-done | bytes 65552 | tf_op jit(solution)/shard_map/reduce_scatter | solution.py:134
  569.5 65.0 %psum.31 = f32[2,128]{1,0:T(2,128)S(1)} all-reduce(f32[2,128]{1,0:T(2,128)S(1)} %pad_maximum_fusion.1), channel_id=1, replica_groups=mesh['row'=16,'col'=8] {'row','col'}, use_global_device_ids=true, to_apply=%region_21.22 | all-reduce | flops 256 | bytes 2048 | tf_op jit(solution)/shard_map/psum | solution.py:142
  636.4 5.1 collective-permute-start.13
  (139 shorter events, 95.5 us)
Async XLA Ops:
  7.2 34.9 %all-gather.5.cloned.1.call-start = ((), (), s32[]{:S(2)}) async-start(), calls=%async_computation.4 | async-start | bytes 3538944 | tf_op jit(solution)/shard_map/all_gather | solution.py:51
  7.9 131.9 %reduce-scatter.5.cloned.1.call-start = ((), (), s32[]{:S(2)}) async-start(), calls=%async_computation.5 | async-start | bytes 2228224 | tf_op jit(solution)/shard_map/reduce_scatter | solution.py:91
  21.0 188.6 %copy-start.5 = (f32[8,16,128]{2,1,0:T(8,128)}, f32[8,16,128]{2,1,0:T(8,128)S(1)}, u32[]{:S(2)}) copy-start(f32[8,16,128]{2,1,0:T(8,128)S(1)} %fusion.82) | copy-start | bytes 196612
  65.3 119.4 %all-gather.7.cloned.1.call-start = ((), (), s32[]{:S(2)}) async-start(), calls=%async_computation.6 | async-start | bytes 1114112 | tf_op jit(solution)/shard_map/all_gather | solution.py:115
  141.3 91.5 %reduce-scatter.7.cloned.1.call-start = ((), (), s32[]{:S(2)}) async-start(), calls=%async_computation.7 | async-start | bytes 589824 | tf_op jit(solution)/shard_map/reduce_scatter | solution.py:134
  203.7 210.3 %reduce-scatter.9.cloned.1.call-start = ((), (), s32[]{:S(2)}) async-start(), calls=%async_computation.8 | async-start | bytes 2228224 | tf_op jit(solution)/shard_map/reduce_scatter | solution.py:91
  204.3 7.0 %collective-permute-start = (bf16[1,128]{1,0:T(2,128)(2,1)}, bf16[1,128]{1,0:T(2,128)(2,1)S(1)}, u32[]{:S(2)}, u32[]{:S(2)}) collective-permute-start(bf16[1,128]{1,0:T(2,128)(2,1)} %get-tuple-element.135), channel_id=1, source_target_pairs={{0,8},{8,16},{16,24},{24,32},{32,40},{40,48},{48,56},{56,64},{64,7... | collective-permute-start | bytes 776 | tf_op jit(solution)/shard_map/ppermute | solution.py:18
  205.5 5.8 collective-permute-start.1
  211.3 4.4 collective-permute-start.3
  212.6 3.8 collective-permute-start.2
  343.0 179.1 %all-gather.9.cloned.1.call-start = ((), (), s32[]{:S(2)}) async-start(), calls=%async_computation.9 | async-start | bytes 1114112 | tf_op jit(solution)/shard_map/all_gather | solution.py:115
  343.1 6.9 %collective-permute-start.4 = (bf16[1,128]{1,0:T(2,128)(2,1)S(1)}, bf16[1,128]{1,0:T(2,128)(2,1)S(1)}, u32[]{:S(2)}, u32[]{:S(2)}) collective-permute-start(bf16[1,128]{1,0:T(2,128)(2,1)S(1)} %get-tuple-element.133), channel_id=1, source_target_pairs={{0,8},{8,16},{16,24},{24,32},{32,40},{40,48},{48,56},{56,64},{64,7... | collective-permute-start | bytes 776 | tf_op jit(solution)/shard_map/ppermute | solution.py:18
  343.3 6.7 %collective-permute-start.5 = (bf16[1,128]{1,0:T(2,128)(2,1)S(1)}, bf16[1,128]{1,0:T(2,128)(2,1)S(1)}, u32[]{:S(2)}, u32[]{:S(2)}) collective-permute-start(bf16[1,128]{1,0:T(2,128)(2,1)S(1)} %get-tuple-element.134), channel_id=1, source_target_pairs={{8,0},{16,8},{24,16},{32,24},{40,32},{48,40},{56,48},{64,56},{72,6... | collective-permute-start | bytes 776 | tf_op jit(solution)/shard_map/ppermute | solution.py:20
  350.0 3.5 collective-permute-start.6
  352.0 3.0 collective-permute-start.7
  483.1 85.5 %reduce-scatter.11.cloned.1.call-start = ((), (), s32[]{:S(2)}) async-start(), calls=%async_computation.10 | async-start | bytes 589824 | tf_op jit(solution)/shard_map/reduce_scatter | solution.py:134
  539.4 6.9 %collective-permute-start.8 = (bf16[1,128]{1,0:T(2,128)(2,1)S(1)}, bf16[1,128]{1,0:T(2,128)(2,1)S(1)}, u32[]{:S(2)}, u32[]{:S(2)}) collective-permute-start(bf16[1,128]{1,0:T(2,128)(2,1)S(1)} %get-tuple-element.131), channel_id=1, source_target_pairs={{0,8},{8,16},{16,24},{24,32},{32,40},{40,48},{48,56},{56,64},{64,7... | collective-permute-start | bytes 776 | tf_op jit(solution)/shard_map/ppermute | solution.py:18
  540.6 5.7 collective-permute-start.9
  546.3 4.4 collective-permute-start.11
  547.7 3.8 collective-permute-start.10
  636.1 6.9 %collective-permute-start.12 = (bf16[1,128]{1,0:T(2,128)(2,1)S(1)}, bf16[1,128]{1,0:T(2,128)(2,1)S(1)}, u32[]{:S(2)}, u32[]{:S(2)}) collective-permute-start(bf16[1,128]{1,0:T(2,128)(2,1)S(1)} %get-tuple-element.129), channel_id=1, source_target_pairs={{0,8},{8,16},{16,24},{24,32},{32,40},{40,48},{48,56},{56,64},{64,7... | collective-permute-start | bytes 776 | tf_op jit(solution)/shard_map/ppermute | solution.py:18
  636.4 6.6 %collective-permute-start.13 = (bf16[1,128]{1,0:T(2,128)(2,1)S(1)}, bf16[1,128]{1,0:T(2,128)(2,1)S(1)}, u32[]{:S(2)}, u32[]{:S(2)}) collective-permute-start(bf16[1,128]{1,0:T(2,128)(2,1)S(1)} %get-tuple-element.130), channel_id=1, source_target_pairs={{8,0},{16,8},{24,16},{32,24},{40,32},{48,40},{56,48},{64,56},{72,6... | collective-permute-start | bytes 776 | tf_op jit(solution)/shard_map/ppermute | solution.py:20
  643.0 4.4 collective-permute-start.15
  644.3 3.8 collective-permute-start.14
  (13 other events, 628.6 us)
Sparse Core Ops, SparseCore 0:
  9.7 32.3 all-gather.4
  65.4 74.2 reduce-scatter.4
  142.7 41.9 all-gather.6
  203.8 28.9 reduce-scatter.6
  343.1 70.9 reduce-scatter.8
  483.2 38.8 all-gather.8
  539.5 29.0 reduce-scatter.10
where the time goes:
time: 658 us; the launch traced here: 656 us
  waiting for transfers between devices  264 us (40%)
  blocking collectives  235 us (36%)
  matrix products  65.4 us (10%)
  starting transfers between devices  37.6 us (6%)
  local copies, waits for them, and re-layouts  25 us (4%)
  other arithmetic  14.6 us (2%)
  between operations  14.4 us (2%)
    reduce_scatter x2, waiting for transfers between devices, apply_transpose(): lax.psum_scatter(partial_value.reshape(-1, experiments), 'row', scatter_d...  133 us
    psum x2, blocking collectives, gradient_total(): return lax.psum(column_sums(vector * vector), ('row', 'col'))  130 us
    all_gather x2, waiting for transfers between devices, per_device(): lax.all_gather(direction.astype(jnp.bfloat16), 'row', axis=0, tiled=True)  82.3 us
    psum x1, blocking collectives, per_device(): totals = lax.psum(pair_sums, ('row', 'col'))  65 us
    reduce_scatter x2, waiting for transfers between devices, per_device(): lax.psum_scatter(forward_partial_value.reshape(-1, experiments).astype(jn...  33.3 us
    all_gather x2, blocking collectives, apply_transpose(): lax.all_gather(vector.astype(jnp.bfloat16), 'col', axis=0, tiled=True)  29.2 us
    ppermute x8, starting transfers between devices, padded_2(): lax.ppermute(head, axis, [((i + 1) % count, i) for i in range(ends)])  24.1 us
    dot_general x2, matrix products, adjoint(): jnp.einsum('ijkq,ijkn->jqn', right_factor, coefficient, preferred_element...  21.5 us
  transfers between devices with their start and end apart: 23, of which 15 were waited for; matrix products, arithmetic and copies ran while one was open for 1% of the time, Pallas kernels for 0%

commit v1 on v0

v1 whole, which is shorter than its diff:
```python
import jax
import jax.numpy as jnp
from jax import lax
from jax.experimental import pallas as pl
from jax.experimental.pallas import tpu as pltpu
from jax.sharding import PartitionSpec as P

F32 = jnp.float32
BF16 = jnp.bfloat16
ROWS = 16
COLS = 8
RANK = 128
RHS = 128
LEAF = 256
BAND = 3
EXTRA = 16
MSG = RHS + EXTRA
ORDER = (1, 3, 2)
FULL = 32000.0
VMEM = pl.BlockSpec(memory_space=pltpu.VMEM)
SMEM = pl.BlockSpec(memory_space=pltpu.SMEM)
HBM = pl.BlockSpec(memory_space=pl.ANY)


def shape(dims, dtype=F32):
    return jax.ShapeDtypeStruct(dims, dtype)


def call(kernel, outs, *args, specs=None, scratch=(), limit=8, flops=0):
    return pl.pallas_call(
        kernel,
        out_shape=outs,
        in_specs=specs or [VMEM] * len(args),
        out_specs=jax.tree.map(lambda _: VMEM, outs),
        scratch_shapes=list(scratch),
        compiler_params=pltpu.CompilerParams(vmem_limit_bytes=limit << 20),
        cost_estimate=pl.CostEstimate(flops=flops, bytes_accessed=1 << 16, transcendentals=0),
    )(*args)


def nt(left, right):
    return lax.dot_general(left, right, (((1,), (1,)), ((), ())), preferred_element_type=F32)


def nn(left, right):
    return jnp.dot(left, right, preferred_element_type=F32)


def row_sum(values):
    folded = values[:, :RHS] + values[:, RHS:]
    return jnp.sum(folded.T, axis=0, keepdims=True)


def as_column(row):
    square = jnp.broadcast_to(row, (RHS, RHS)).T
    return jnp.concatenate([square, square], axis=1)


def split3(row):
    high = row.astype(BF16).astype(F32)
    middle = (row - high).astype(BF16).astype(F32)
    return [high, middle, row - high - middle]


def code_of(largest):
    return jnp.ceil(jnp.log2(jnp.maximum(largest, 1e-30)) * 128.0)


def size_of(code):
    return jnp.exp2(code * (1.0 / 128.0))


def to_int16(values):
    return jnp.round(values).astype(jnp.int32).astype(jnp.int16)


def encode_rows(sums):
    rows = []
    for value in sums:
        code = code_of(jnp.abs(value))
        scaled = value / size_of(code) * FULL
        whole = jnp.round(scaled)
        rows += [code, whole, jnp.round((scaled - whole) * 65000.0)]
    return rows


def decode_rows(extra):
    rows = extra[...].astype(jnp.int32).astype(F32)[:, :RHS]
    sums = []
    for at in (4, 7):
        whole = rows[at + 1 : at + 2] + rows[at + 2 : at + 3] * (1.0 / 65000.0)
        sums.append(size_of(rows[at : at + 1]) * whole * (1.0 / FULL))
    return sums


def encode(out, pieces, sums):
    lane = lax.broadcasted_iota(jnp.int32, (RHS, RHS), 1)
    codes = jnp.zeros((RHS, RHS), F32)
    for m, piece in enumerate(pieces):
        code = code_of(jnp.max(jnp.abs(piece), axis=1, keepdims=True))
        out[m * RHS : (m + 1) * RHS] = to_int16(piece * (FULL / size_of(code)))
        codes = jnp.where(lane == m, code, codes)
    rows = jnp.concatenate([codes.T[:4]] + encode_rows(sums) + [jnp.zeros((EXTRA - 10, RHS), F32)], axis=0)
    out[len(pieces) * RHS :] = to_int16(jnp.concatenate([rows, jnp.zeros_like(rows)], axis=1))


def decode(message, count):
    rows = message[count * RHS :].astype(jnp.int32).astype(F32)[:, :RHS]
    square = jnp.concatenate([rows, jnp.zeros((RHS - EXTRA, RHS), F32)], axis=0).T
    pieces = []
    for m in range(count):
        scale = size_of(square[:, m : m + 1]) * (1.0 / FULL)
        pieces.append(message[m * RHS : (m + 1) * RHS].astype(jnp.int32).astype(F32) * scale)
    return pieces


def two_rows(rows):
    return jnp.concatenate([rows[0], rows[1], jnp.zeros((6, RHS), F32)], axis=0)


def live_pair(live, leaf_a, leaf_b):
    return jnp.concatenate([live[pl.ds(leaf_a, 1), :], live[pl.ds(leaf_b, 1), :]], axis=1)


def first_message(data, extra, out):
    out[:RHS] = data[...].T.astype(BF16)
    out[RHS:] = extra[...]


M_ROW, M_HALO, M_OWNER, M_AT, M_ODD, M_COL = 16, 24, 26, 27, 28, 29


def slot_of(meta, column):
    apart = column ^ meta[M_AT]
    swapped = (apart % 4) * 4 + apart // 4
    return jnp.where(meta[M_ODD] == 1, swapped, apart)


def tile_at(tiles, s, k):
    return tiles[s % 4][BAND * (s // 4) + k]


def data_pieces(group, other):
    return [a[:RHS] for a in group] + [other[MSG * m : MSG * m + RHS] for m in range(4)]


def data_extras(group, other):
    return [a[RHS:] for a in group] + [other[MSG * m + RHS : MSG * (m + 1)] for m in range(4)]


def add_near_terms(meta, cols, pieces, tiles, near):
    near[...] = jnp.zeros_like(near)

    @pl.when(meta[M_OWNER] == 1)
    def _():
        for s in range(COLS):
            for k in range(BAND):
                slot = slot_of(meta, cols[s, k])
                near[slot] += nn(pieces[s], tile_at(tiles, s, k))


def far_pair(meta, live, left, right, pieces, slot):
    ja, jb = meta[slot], meta[slot + 1]
    coef_a, coef_b, right_a, right_b = [], [], [], []
    for s in range(COLS):
        base = meta[M_ROW + s] * ROWS
        pair = jnp.concatenate([left[base + ja], left[base + jb]], axis=0)
        coef = (nt(pieces[s], pair) * live_pair(live, base + ja, base + jb)).astype(BF16)
        coef_a.append(coef[:, :RANK])
        coef_b.append(coef[:, RANK:])
        right_a.append(right[base + ja])
        right_b.append(right[base + jb])
    part_a = nn(jnp.concatenate(coef_a, axis=1), jnp.concatenate(right_a, axis=0))
    part_b = nn(jnp.concatenate(coef_b, axis=1), jnp.concatenate(right_b, axis=0))
    return part_a, part_b


def far_group(meta, live, left, right, pieces, m2):
    first = far_pair(meta, live, left, right, pieces, 4 * m2)
    return first + far_pair(meta, live, left, right, pieces, 4 * m2 + 2)


def far_only_kernel(meta, live, left, right, a0, a1, a2, a3, b, far, cols):
    pieces = data_pieces((a0, a1, a2, a3), b)
    rows = [extra.astype(F32)[:1, :RHS] for extra in data_extras((a0, a1, a2, a3), b)]
    cols[...] = jnp.concatenate(rows, axis=0).astype(jnp.int32)
    for m2 in range(4):
        for m1, part in enumerate(far_group(meta, live, left, right, pieces, m2)):
            far[4 * m2 + m1] = part


def near_encode_kernel(meta, cols, far, a0, a1, a2, a3, b, t0, t1, t2, t3, g1, g3, g2, own_out, near):
    add_near_terms(meta, cols, data_pieces((a0, a1, a2, a3), b), (t0, t1, t2, t3), near)
    zero = jnp.zeros((1, RHS), F32)
    for m2, out in ((1, g1), (3, g3), (2, g2)):
        encode(out, [far[4 * m2 + m] + near[4 * m2 + m] for m in range(4)], [zero, zero])
    for m in range(4):
        own_out[m * RHS : (m + 1) * RHS] = far[m] + near[m]


def adjoint_first_kernel(
    meta, cols, reg, live, left, right, a0, a1, a2, a3, b, t0, t1, t2, t3, g1, g3, g2, near, sums_out, rims_out, first, last
):
    pieces = data_pieces((a0, a1, a2, a3), b)
    sums = [jnp.zeros((1, RHS), F32)] * 2
    for s, extra in enumerate(data_extras((a0, a1, a2, a3), b)):
        terms = extra.astype(F32)[:, :RHS]
        sums = [sums[0] + (terms[0:1] + terms[1:2] + terms[2:3]), sums[1] + (terms[3:4] + terms[4:5] + terms[5:6])]
        column = meta[M_ROW + s]
        first[pl.ds(column, 1), :] = terms[6:7]
        last[pl.ds(column, 1), :] = terms[7:8]
    at, column = meta[M_AT], meta[M_COL]
    cross = jnp.sum(last[0 : COLS - 1] * first[1:COLS], axis=0, keepdims=True)
    sums[1] += jnp.where(at == 0, -2.0 * reg[...] * cross, 0.0)
    before = last[pl.ds(jnp.maximum(column - 1, 0), 1), :]
    after = first[pl.ds(jnp.minimum(column + 1, COLS - 1), 1), :]
    rims_out[...] = two_rows(
        [
            jnp.where(column > 0, before, 0.0),
            jnp.where(column < COLS - 1, after, 0.0),
        ]
    )
    sums_out[...] = two_rows(sums)
    add_near_terms(meta, cols, pieces, (t0, t1, t2, t3), near)
    for m2, out in ((1, g1), (3, g3), (2, g2)):
        parts = far_group(meta, live, left, right, pieces, m2)
        encode(out, [part + near[4 * m2 + m] for m, part in enumerate(parts)], sums)


def adjoint_second_kernel(meta, live, left, right, a0, a1, a2, a3, b, near, own_out):
    pieces = data_pieces((a0, a1, a2, a3), b)
    for m, part in enumerate(far_group(meta, live, left, right, pieces, 0)):
        own_out[m * RHS : (m + 1) * RHS] = part + near[m]


def coefficient_pair(meta, live, right, held, s, slots):
    base_a, base_b = meta[M_ROW + s] * ROWS, meta[M_ROW + s + 1] * ROWS
    coef_a, coef_b = [], []
    for slot in slots:
        j = meta[slot]
        pair = jnp.concatenate([right[base_a + j], right[base_b + j]], axis=0)
        coef = (nt(held(slot), pair) * live_pair(live, base_a + j, base_b + j)).astype(BF16)
        coef_a.append(coef[:, :RANK])
        coef_b.append(coef[:, RANK:])
    return jnp.concatenate(coef_a, axis=1), jnp.concatenate(coef_b, axis=1)


def piece_of(arrays):
    def held(slot):
        return arrays[slot // 4][(slot % 4) * RHS : (slot % 4 + 1) * RHS]

    return held


def coefficient_kernel(meta, live, right, a, coef):
    for s in (4, 6, 0, 2):
        coef[s], coef[s + 1] = coefficient_pair(meta, live, right, piece_of((a,)), s, range(4))


def forward_rows(meta, cols, live, left, right, coef, arrays, tiles, out, near, held, start):
    piece = piece_of(arrays)
    for slot in range(ROWS):
        held[slot] = piece(slot)
    near[...] = jnp.zeros_like(near)

    @pl.when(meta[M_OWNER] == 1)
    def _():
        for m in range(4):
            for k in range(BAND):
                slot = slot_of(meta, cols[start + m, k])
                near[m] += nt(held[slot], tile_at(tiles, start + m, k))

    for m in (0, 2):
        s = start + m
        more = coefficient_pair(meta, live, right, piece, s, range(4, ROWS))
        for at in range(2):
            base = meta[M_ROW + s + at] * ROWS
            factor = jnp.concatenate([left[base + meta[slot]] for slot in range(ROWS)], axis=0)
            value = nn(jnp.concatenate([coef[s + at], more[at]], axis=1), factor) + near[m + at]
            out[(m + at) * RHS : (m + at + 1) * RHS] = value.astype(out.dtype)


def forward_first_kernel(
    meta, cols, live, left, right, coef, a, b1, b2, b3, t0, t1, t2, t3, out, held, near
):
    forward_rows(
        meta, cols, live, left, right, coef, (a, b1, b2, b3), (t0, t1, t2, t3), out, near, held, 4
    )


def forward_second_kernel(
    meta, cols, live, left, right, coef, a, b1, b2, b3, t0, t1, t2, t3, own, out, curved, edges, held, near
):
    forward_rows(
        meta, cols, live, left, right, coef, (a, b1, b2, b3), (t0, t1, t2, t3), out, near, held, 0
    )
    lane = lax.broadcasted_iota(jnp.int32, (RHS, LEAF), 1)
    for m in range(4):
        rows = slice(m * RHS, (m + 1) * RHS)
        vector, j = own[rows], meta[m]
        before = held[slot_of(meta, (j + ROWS - 1) % ROWS)][:, LEAF - RHS :].astype(F32)[:, RHS - 1 :]
        after = held[slot_of(meta, (j + 1) % ROWS)][:, :RHS].astype(F32)[:, :1]
        before = jnp.where(j == 0, 0.0, before)
        after = jnp.where(j == ROWS - 1, 0.0, after)
        below = jnp.where(lane == 0, before, pltpu.roll(vector, 1, 1))
        above = jnp.where(lane == LEAF - 1, after, pltpu.roll(vector, LEAF - 1, 1))
        curved[rows] = 2.0 * vector - below - above
    first = held[slot_of(meta, 0)][:, :RHS].astype(F32).T[:1]
    last = held[slot_of(meta, ROWS - 1)][:, LEAF - RHS :].astype(F32).T[RHS - 1 :]
    edges[...] = two_rows([first, last])


def without_rims(curved, before, after, j):
    lane = lax.broadcasted_iota(jnp.int32, (RHS, LEAF), 1)
    curved = curved - jnp.where((lane == 0) & (j == 0), before, 0.0)
    return curved - jnp.where((lane == LEAF - 1) & (j == ROWS - 1), after, 0.0)


def row_phase_kernel(own, sums_in, g1, g3, g2, own_out, sums_out, message):
    sums = [sums_in[0:1], sums_in[1:2]]
    totals = [own[m * RHS : (m + 1) * RHS] for m in range(4)]
    for g in (g1, g3, g2):
        sums = [x + y for x, y in zip(sums, decode_rows(g[4 * RHS :]))]
        totals = [x + y for x, y in zip(totals, decode(g, 4))]
    sums_out[...] = two_rows(sums)
    encode(message, totals, sums)
    for m in range(4):
        own_out[m * RHS : (m + 1) * RHS] = totals[m]


def group_totals(own, p1, p3, p2):
    totals = [own[m * RHS : (m + 1) * RHS] for m in range(4)]
    for k, p in ((1, p1), (3, p3), (2, p2)):
        got = decode(p, 4)
        totals = [total + got[k ^ m] for m, total in enumerate(totals)]
    return totals


def descent_kernel(own, p1, p3, p2, full, sent):
    for m, total in enumerate(group_totals(own, p1, p3, p2)):
        full[m * RHS : (m + 1) * RHS] = total
        sent[m * RHS : (m + 1) * RHS] = total.astype(BF16)


def descent2_kernel(meta, reg, first, curved, rims, own, sums_in, p1, p3, p2, full, sent, curved_out, sums_out):
    sums = [sums_in[0:1], sums_in[1:2]]
    for p in (p1, p3, p2):
        sums = [x + y for x, y in zip(sums, decode_rows(p[4 * RHS :]))]
    sums_out[...] = two_rows(sums)
    step, weight = as_column(sums[0] / sums[1]), as_column(reg[...])
    before, after = as_column(rims[0:1]), as_column(rims[1:2])
    for m, total in enumerate(group_totals(own, p1, p3, p2)):
        rows = slice(m * RHS, (m + 1) * RHS)
        whole = without_rims(curved[rows], before, after, meta[m])
        curved_out[rows] = whole
        vector = first[rows] - step * (total + weight * whole)
        full[rows] = vector
        sent[rows] = vector.astype(BF16)


def core_phase_kernel(own, other, own_out, p1, p3, p2):
    for m, out in ((1, p1), (3, p3), (2, p2), (0, own_out)):
        rows = slice(m * RHS, (m + 1) * RHS)
        out[...] = (own[rows] + other[rows].astype(F32)).astype(out.dtype)


def image_kernel(reg, vector, curved, edges, own, p1, p3, p2, full, message):
    total = own[...]
    for p in (p1, p3, p2):
        total += p[...].astype(F32)
    full[...] = total
    value = vector[:RHS]
    message[:RHS] = total.astype(BF16)
    gamma = row_sum(value * value)
    delta = row_sum(total * total) + reg[...] * row_sum(value * curved[:RHS])
    rows = jnp.concatenate(
        split3(gamma) + split3(delta) + [edges[0:2], jnp.zeros((EXTRA - 8, RHS), F32)], axis=0
    )
    message[RHS:] = jnp.concatenate([rows, jnp.zeros_like(rows)], axis=1).astype(BF16)


def image2_kernel(meta, reg, vector, curved, edges, curved_first, first, own, p1, p3, p2, full, sums):
    total = own[...]
    for p in (p1, p3, p2):
        total += p[...].astype(F32)
    full[...] = total
    value = vector[:RHS]
    weight = reg[...]
    sums[...] = jnp.zeros_like(sums)
    sums[0:1] = row_sum(value * value)
    sums[1:2] = row_sum(total * total) + weight * row_sum(value * curved[:RHS])
    sums[2:3] = row_sum(total * first[...]) + weight * row_sum(value * curved_first[:RHS])
    column = meta[M_COL]
    sums[pl.ds(8 + column, 1), :] = jnp.where(meta[M_AT] == 0, edges[0:1], 0.0)
    sums[pl.ds(16 + column, 1), :] = jnp.where(meta[M_AT] == 0, edges[1:2], 0.0)


def final_kernel(meta, reg, sums1, sums2, s1, s2, d1, d2, y1, y2, data, solution_out, misfit_out, curved_out):
    gamma, delta = sums1[0:1], sums1[1:2]
    first, last = sums2[8 : 8 + COLS], sums2[16 : 16 + COLS]
    cross = jnp.sum(last[: COLS - 1] * first[1:], axis=0, keepdims=True)
    fresh, delta_new, delta_mixed = sums2[0:1], sums2[1:2] - 2.0 * reg[...] * cross, sums2[2:3]
    column = meta[M_COL]
    before = sums2[pl.ds(16 + jnp.maximum(column - 1, 0), 1), :]
    after = sums2[pl.ds(8 + jnp.minimum(column + 1, COLS - 1), 1), :]
    rims = [
        jnp.where(column > 0, before, 0.0),
        jnp.where(column < COLS - 1, after, 0.0),
    ]
    beta = fresh / gamma
    delta2 = delta_new + 2.0 * beta * delta_mixed + beta * beta * delta
    step2 = fresh / delta2
    one = as_column(gamma / delta + step2 * beta)
    two = as_column(step2)
    whole = without_rims(d2[:RHS], as_column(rims[0]), as_column(rims[1]), meta[M_AT])
    solution_out[...] = (one * s1[:RHS] + two * s2[:RHS]).T
    curved_out[...] = (one * d1[:RHS] + two * whole).T
    misfit_out[...] = data[...] - (one * y1[...] + two * y2[...]).T


def grid_pairs(move):
    return [(r * COLS + c, to) for r in range(ROWS) for c in range(COLS) for to in [move(r, c)] if to is not None]


def send(value, move):
    return lax.ppermute(value, ("row", "col"), grid_pairs(move))


def near_move(m):
    return lambda r, c: (r ^ (m if c % 2 == 0 else 4 * m)) * COLS + c


def far_move(m):
    return lambda r, c: (r ^ (4 * m if c % 2 == 0 else m)) * COLS + c


def y_move(m):
    return lambda r, c: r * COLS + (c ^ (2 * m))


def core_move(r, c):
    return r * COLS + (c ^ 1)


def tile_core_move(r, c):
    return r * COLS + (c ^ 1) if c % 2 != (r // 2) % 2 else None


def tile_move(m):
    def move(r, c):
        owner = r // 2
        there = c % 2 == owner % 2 and (c // 2) ^ (owner // 2) == m
        return r * COLS + (c ^ (2 * m)) if there else None

    return move


def per_device(far_left, far_right, far_rank, near_tiles, near_cols, data, reg_weight):
    r = lax.axis_index("row")
    c = lax.axis_index("col")
    odd = c % 2
    leaves = far_rank.shape[-1]

    def at_slot(m2, m1):
        return jnp.where(odd == 0, r ^ m1 ^ (4 * m2), r ^ (4 * m1) ^ m2)

    def slot_at(column):
        apart = column ^ r
        return jnp.where(odd == 1, (apart % 4) * 4 + apart // 4, apart)

    meta = jnp.stack(
        [at_slot(s // 4, s % 4) for s in range(ROWS)]
        + [c ^ (2 * (s % 4)) ^ (s // 4) for s in range(COLS)]
        + [slot_at((r + ROWS - 1) % ROWS), slot_at((r + 1) % ROWS)]
        + [(c == r // 2).astype(jnp.int32), r, odd, c]
    ).astype(jnp.int32)
    reg = reg_weight.reshape(1, RHS)
    data = data.reshape(LEAF, RHS)

    cols_row = jnp.pad(near_cols.astype(BF16), ((0, EXTRA - 1), (0, LEAF - BAND)))
    message = call(first_message, shape((MSG, LEAF), BF16), data, cols_row)

    def gather_col_pieces(mine):
        got = {m: send(mine, y_move(m)) for m in ORDER}
        return [mine, got[1], got[2], got[3]]

    group = gather_col_pieces(message)
    tiles, _ = lax.optimization_barrier((near_tiles.reshape(BAND, LEAF, LEAF), message))
    tiles = jnp.concatenate([tiles, send(tiles, tile_core_move)], axis=0)
    tiles, _ = lax.optimization_barrier((tiles, group))
    tiles = [tiles] + [send(tiles, tile_move(m)) for m in (1, 2, 3)]
    left = far_left.reshape(leaves, RANK, LEAF)
    right = far_right.reshape(leaves, RANK, LEAF)
    live = (lax.broadcasted_iota(jnp.int32, (leaves, RANK), 1) < far_rank.reshape(leaves, 1)).astype(F32)
    other = send(jnp.concatenate(group, axis=0), core_move)

    def factors():
        return [live] + [pltpu.with_memory_space_constraint(x, pltpu.VMEM) for x in (left, right)]

    vec, sums_shape = shape((RHS, LEAF)), shape((8, RHS))
    sent_shape = shape((RHS, LEAF), BF16)
    group4, group4_sent = shape((4 * RHS, LEAF)), shape((4 * RHS, LEAF), BF16)
    big = shape((4 * RHS + EXTRA, LEAF), jnp.int16)
    near_shape = shape((ROWS, RHS, LEAF))
    near_scratch = pltpu.VMEM((ROWS, RHS, LEAF), F32)

    def specs(scalars, vectors):
        return [SMEM] * scalars + [VMEM] * vectors

    def sum_over_row(own, sums, parts):
        got = [send(g, far_move(m)) for m, g in zip(ORDER, parts)]
        own, sums, message = call(row_phase_kernel, (group4, sums_shape, big), own, sums, *got)
        return own, sums, [send(message, near_move(m)) for m in ORDER]

    def product(vector, sent):
        got = {m: send(sent, far_move(m)) for m in ORDER}
        pieces = [sent, got[1], got[2], got[3]]
        coef = call(
            coefficient_kernel, shape((COLS, RHS, 4 * RANK), BF16), meta, live, factors()[2], sent,
            specs=specs(1, 3), flops=1 << 28,
        )
        scratch = [pltpu.VMEM((ROWS, RHS, LEAF), BF16), pltpu.VMEM((4, RHS, LEAF), F32)]
        parts = call(
            forward_first_kernel, group4_sent, meta, cols, *factors(), coef, *pieces, *tiles,
            specs=specs(2, 12), scratch=scratch, flops=1 << 30,
        )
        other = send(parts, core_move)
        own, curved, edges = call(
            forward_second_kernel, (group4, group4, sums_shape), meta, cols, *factors(), coef, *pieces, *tiles, vector,
            specs=specs(2, 13), scratch=scratch, flops=1 << 30,
        )
        own, p1, p3, p2 = call(core_phase_kernel, (vec, sent_shape, sent_shape, sent_shape), own, other)
        return curved, edges, [own] + [send(p, y_move(m)) for m, p in zip(ORDER, (p1, p3, p2))]

    far, cols = call(
        far_only_kernel, (near_shape, shape((COLS, RHS), jnp.int32)), meta, *factors(), *group, other,
        specs=specs(1, 8), flops=1 << 31,
    )
    g1, g3, g2, own = call(
        near_encode_kernel, (big, big, big, group4), meta, cols, far, *group, other, *tiles,
        specs=specs(2, 10), scratch=[near_scratch], flops=1 << 29,
    )
    own, _, parts = sum_over_row(own, jnp.zeros((8, RHS), F32), (g1, g3, g2))
    s1, s1_sent = call(descent_kernel, (group4, group4_sent), own, *parts)
    d1, edges, parts = product(s1, s1_sent)
    y1, message = call(image_kernel, (vec, shape((MSG, LEAF), BF16)), reg, s1, d1, edges, *parts)

    group = gather_col_pieces(message)
    other = send(jnp.concatenate(group, axis=0), core_move)
    g1, g3, g2, near, sums, rims = call(
        adjoint_first_kernel, (big, big, big, near_shape, sums_shape, sums_shape),
        meta, cols, reg, *factors(), *group, other, *tiles,
        specs=specs(2, 13), scratch=[pltpu.VMEM((COLS, RHS), F32)] * 2, flops=1 << 30,
    )
    own = call(
        adjoint_second_kernel, group4, meta, *factors(), *group, other, near,
        specs=specs(1, 9), flops=1 << 30,
    )
    own, sums, parts = sum_over_row(own, sums, (g1, g3, g2))
    s2, s2_sent, d1, sums1 = call(
        descent2_kernel, (group4, group4_sent, group4, sums_shape), meta, reg, s1, d1, rims, own, sums, *parts,
        specs=specs(1, 9),
    )
    d2, edges, parts = product(s2, s2_sent)
    y2, sums2 = call(
        image2_kernel, (vec, shape((24, RHS))), meta, reg, s2, d2, edges, d1, y1, *parts, specs=specs(1, 10)
    )
    sums2 = sums2 + send(sums2, core_move)
    for move in (y_move, near_move, far_move):
        got = {m: send(sums2, move(m)) for m in ORDER}
        sums2 = (sums2 + got[1]) + (got[2] + got[3])
    piece = shape((LEAF, RHS))
    solution_out, misfit_out, curved_out = call(
        final_kernel, (piece, piece, piece), meta, reg, sums1, sums2, s1, s2, d1, d2, y1, y2, data, specs=specs(1, 10)
    )
    whole = (1, 1, LEAF, RHS)
    return solution_out.reshape(whole), misfit_out.reshape(whole), curved_out.reshape(whole)


def solution(mesh):
    in_specs = (
        P("row", "col", None, None, None),
        P("row", "col", None, None, None),
        P("row", "col", None),
        P(("row", "col"), None, None, None),
        P(("row", "col"), None),
        P("row", "col", None, None),
        P(),
    )
    out_specs = (
        P("col", "row", None, None),
        P("row", "col", None, None),
        P("col", "row", None, None),
    )
    return jax.shard_map(
        per_device, mesh=mesh, in_specs=in_specs, out_specs=out_specs, check_vma=False
    )
```

time: 658 us -> 177 us (0.27)
  blocking collectives: 235 us -> 0 us
  waiting for transfers between devices: 264 us -> 66.4 us
  matrix products: 65.4 us -> 0 us
  Pallas kernels: 0 us -> 35.1 us
  starting transfers between devices: 37.6 us -> 59.6 us
  local copies, waits for them, and re-layouts: 25 us -> 11.1 us
  between operations: 14.4 us -> 0.95 us
  other arithmetic: 14.6 us -> 3.26 us
    psum x3 -> x0, blocking collectives: 195 us -> none  [the longest x2 130 us: gradient_total(): return lax.psum(column_sums(vector * vector), ('row', 'col'))]
    reduce_scatter x4 -> x0, waiting for transfers between devices: 166 us -> none  [the longest x2 133 us: apply_transpose(): lax.psum_scatter(partial_value.reshape(-1, experiments), 'row', scatter_d...]
    all_gather x3 -> x0, waiting for transfers between devices: 87.3 us -> none  [the longest x2 82.3 us: per_device(): lax.all_gather(direction.astype(jnp.bfloat16), 'row', axis=0, tiled=True)]
    dot_general x10 -> x0, matrix products: 65.4 us -> none  [the longest x2 21.5 us: adjoint(): jnp.einsum('ijkq,ijkn->jqn', right_factor, coefficient, preferred_element...]
    ppermute x16 -> x48, waiting for transfers between devices: 9.36 us -> 66.4 us  [send(): return lax.ppermute(value, ('row', 'col'), grid_pairs(move))]
    all_gather x3 -> x0, blocking collectives: 40.2 us -> none  [the longest x2 29.2 us: apply_transpose(): lax.all_gather(vector.astype(jnp.bfloat16), 'col', axis=0, tiled=True)]
    pallas_call x0 -> x20, Pallas kernels: none -> 35.1 us  [call(): pl.pallas_call(kernel, out_shape=outs, in_specs=specs or [VMEM] * len(arg...]
    ppermute x16 -> x48, starting transfers between devices: 37.3 us -> 59.6 us  [send(): return lax.ppermute(value, ('row', 'col'), grid_pairs(move))]
  transfers between devices with their start and end apart: 23 -> 48, of which waited for: 15 -> 37; matrix products, arithmetic and copies ran while one was open for 1% -> 2% of each run, Pallas kernels for 0% -> 9%
where the time goes in v1:
time: 177 us; the launch traced here: 176 us
  waiting for transfers between devices  66.4 us (38%)
  starting transfers between devices  59.6 us (34%)
  Pallas kernels  35.1 us (20%)
  local copies, waits for them, and re-layouts  11.1 us (6%)
  other arithmetic  3.26 us (2%)
    ppermute x48, waiting for transfers between devices, send(): return lax.ppermute(value, ('row', 'col'), grid_pairs(move))  66.4 us
    ppermute x48, starting transfers between devices, send(): return lax.ppermute(value, ('row', 'col'), grid_pairs(move))  59.6 us
    pallas_call x20, Pallas kernels, call(): pl.pallas_call(kernel, out_shape=outs, in_specs=specs or [VMEM] * len(arg...  35.1 us
    unnamed x28, local copies, waits for them, and re-layouts  11 us
  transfers between devices with their start and end apart: 48, of which 37 were waited for; matrix products, arithmetic and copies ran while one was open for 2% of the time, Pallas kernels for 9%

profile of v1, /device:TPU:0, one launch (start us, length us, event | category | flops | bytes accessed | tf_op | source)
XLA Modules:
  0.0 176.3 jit_solution(6151218560083489902)
XLA Ops:
  3.6 3.2 %collective-permute-start.2 = (bf16[144,256]{1,0:T(8,128)(2,1)S(1)}, bf16[144,256]{1,0:T(8,128)(2,1)S(1)}, u32[]{:S(2)}, u32[]{:S(2)}) collective-permute-start(bf16[144,256]{1,0:T(8,128)(2,1)S(1)} %shard_map.94.a0), channel_id=1, source_target_pairs={{0,6},{1,7},{2,4},{3,5},{4,2},{5,3},{6,0},{7,1},{8,14},{9,15},{10,... | collective-permute-start | bytes 221192 | tf_op jit(solution)/shard_map/ppermute | solution.py:426
  10.7 2.7 %collective-permute-done.1.a2 = bf16[144,256]{1,0:T(8,128)(2,1)S(1)} collective-permute-done((bf16[144,256]{1,0:T(8,128)(2,1)S(1)}, bf16[144,256]{1,0:T(8,128)(2,1)S(1)}, u32[]{:S(2)}, u32[]{:S(2)}) %collective-permute-start.1) | collective-permute-done | bytes 73760 | tf_op jit(solution)/shard_map/ppermute | solution.py:426
  20.5 3.4 %copy-done = bf16[1,1,128,128,256]{4,3,2,1,0:T(8,128)(2,1)S(1)} copy-done((bf16[1,1,128,128,256]{4,3,2,1,0:T(8,128)(2,1)S(1)}, bf16[1,1,128,128,256]{4,3,2,1,0:T(8,128)(2,1)}, u32[]{:S(2)}) %copy-start) | copy-done | bytes 8388632
  23.9 3.4 %copy-done.2 = bf16[1,1,128,128,256]{4,3,2,1,0:T(8,128)(2,1)S(1)} copy-done((bf16[1,1,128,128,256]{4,3,2,1,0:T(8,128)(2,1)S(1)}, bf16[1,1,128,128,256]{4,3,2,1,0:T(8,128)(2,1)}, u32[]{:S(2)}) %copy-start.2) | copy-done | bytes 8388632
  29.9 4.7 %shard_map.95 = (f32[16,128,256]{2,1,0:T(8,128)S(1)}, s32[8,128]{1,0:T(8,128)S(1)}) custom-call(s32[30]{0:T(128)S(1)} %stack.121.meta, f32[128,128]{1,0:T(8,128)S(1)} %fusion.live, bf16[128,128,256]{2,1,0:T(8,128)(2,1)S(1)} %bitcast.46, bf16[128,128,256]{2,1,0:T(8,128)(2,1)S(1)} %bitcast.37, bf16[144,256]{1,0:T(8,128)(2,1)S(1)} %shard_map.94.a0, ...), custom_call_target="tpu_custom_call" | custom-call | flops 2147483648 | bytes 65536 | tf_op jit(solution)/shard_map/pallas_call | solution.py:30
  39.0 3.0 %collective-permute-start.9 = (s16[528,256]{1,0:T(8,128)(2,1)S(1)}, s16[528,256]{1,0:T(8,128)(2,1)S(1)}, u32[]{:S(2)}, u32[]{:S(2)}) collective-permute-start(s16[528,256]{1,0:T(8,128)(2,1)S(1)} %get-tuple-element.55), channel_id=1, source_target_pairs={{0,96},{1,25},{2,98},{3,27},{4,100},{5,29},{6,102},{7,31},{8,104},... | collective-permute-start | bytes 811016 | tf_op jit(solution)/shard_map/ppermute | solution.py:426
  45.5 3.4 %collective-permute-done.9.g3 = s16[528,256]{1,0:T(8,128)(2,1)S(1)} collective-permute-done((s16[528,256]{1,0:T(8,128)(2,1)S(1)}, s16[528,256]{1,0:T(8,128)(2,1)S(1)}, u32[]{:S(2)}, u32[]{:S(2)}) %collective-permute-start.9) | collective-permute-done | bytes 270368 | tf_op jit(solution)/shard_map/ppermute | solution.py:426
  51.8 3.9 %collective-permute-start.12 = (s16[528,256]{1,0:T(8,128)(2,1)S(1)}, s16[528,256]{1,0:T(8,128)(2,1)S(1)}, u32[]{:S(2)}, u32[]{:S(2)}) collective-permute-start(s16[528,256]{1,0:T(8,128)(2,1)S(1)} %get-tuple-element.58), channel_id=1, source_target_pairs={{0,24},{1,97},{2,26},{3,99},{4,28},{5,101},{6,30},{7,103},{8,16},{... | collective-permute-start | bytes 811016 | tf_op jit(solution)/shard_map/ppermute | solution.py:426
  55.8 3.5 %collective-permute-done.13.p2 = s16[528,256]{1,0:T(8,128)(2,1)S(1)} collective-permute-done((s16[528,256]{1,0:T(8,128)(2,1)S(1)}, s16[528,256]{1,0:T(8,128)(2,1)S(1)}, u32[]{:S(2)}, u32[]{:S(2)}) %collective-permute-start.13) | collective-permute-done | bytes 270368 | tf_op jit(solution)/shard_map/ppermute | solution.py:426
  59.3 2.8 %collective-permute-done.12.p3 = s16[528,256]{1,0:T(8,128)(2,1)S(1)} collective-permute-done((s16[528,256]{1,0:T(8,128)(2,1)S(1)}, s16[528,256]{1,0:T(8,128)(2,1)S(1)}, u32[]{:S(2)}, u32[]{:S(2)}) %collective-permute-start.12) | collective-permute-done | bytes 270368 | tf_op jit(solution)/shard_map/ppermute | solution.py:426
  62.7 2.7 %collective-permute-start.16 = (bf16[512,256]{1,0:T(8,128)(2,1)S(1)}, bf16[512,256]{1,0:T(8,128)(2,1)S(1)}, u32[]{:S(2)}, u32[]{:S(2)}) collective-permute-start(bf16[512,256]{1,0:T(8,128)(2,1)S(1)} %get-tuple-element.60.a), channel_id=1, source_target_pairs={{0,96},{1,25},{2,98},{3,27},{4,100},{5,29},{6,102},{7,31},{8,104},... | collective-permute-start | bytes 786440 | tf_op jit(solution)/shard_map/ppermute | solution.py:426
  68.2 3.8 %collective-permute-done.16.b3 = bf16[512,256]{1,0:T(8,128)(2,1)S(1)} collective-permute-done((bf16[512,256]{1,0:T(8,128)(2,1)S(1)}, bf16[512,256]{1,0:T(8,128)(2,1)S(1)}, u32[]{:S(2)}, u32[]{:S(2)}) %collective-permute-start.16) | collective-permute-done | bytes 262176 | tf_op jit(solution)/shard_map/ppermute | solution.py:426
  74.1 3.3 %shard_map.101 = bf16[512,256]{1,0:T(8,128)(2,1)S(1)} custom-call(s32[30]{0:T(128)S(1)} %stack.121.meta, s32[8,128]{1,0:T(8,128)S(1)} %get-tuple-element.49.cols, f32[128,128]{1,0:T(8,128)S(1)} %fusion.live, bf16[128,128,256]{2,1,0:T(8,128)(2,1)S(1)} %bitcast.49, bf16[128,128,256]{2,1,0:T(8,128)(2,1)S(1)} %bitcast.39, ...), custom_call_target="tpu_custom_call" | custom-call | flops 1073741824 | bytes 65536 | tf_op jit(solution)/shard_map/pallas_call | solution.py:30
  77.5 3.2 %shard_map.100 = (f32[512,256]{1,0:T(8,128)S(1)}, f32[512,256]{1,0:T(8,128)S(1)}, f32[8,128]{1,0:T(8,128)S(1)}) custom-call(s32[30]{0:T(128)S(1)} %stack.121.meta, s32[8,128]{1,0:T(8,128)S(1)} %get-tuple-element.49.cols, f32[128,128]{1,0:T(8,128)S(1)} %fusion.live, bf16[128,128,256]{2,1,0:T(8,128)(2,1)S(1)} %bitcast.50, bf16[128,128,256]{2,1,0:T(8,128)(2,1)S(1)} %bitcast.40, ...), custom_call_target="tpu_custom_call" | custom-call | flops 1073741824 | bytes 65536 | tf_op jit(solution)/shard_map/pallas_call | solution.py:30
  82.4 2.6 %collective-permute-start.20 = (bf16[128,256]{1,0:T(8,128)(2,1)S(1)}, bf16[128,256]{1,0:T(8,128)(2,1)S(1)}, u32[]{:S(2)}, u32[]{:S(2)}) collective-permute-start(bf16[128,256]{1,0:T(8,128)(2,1)S(1)} %get-tuple-element.67), channel_id=1, source_target_pairs={{0,4},{1,5},{2,6},{3,7},{4,0},{5,1},{6,2},{7,3},{8,12},{9,13},{10,... | collective-permute-start | bytes 196616 | tf_op jit(solution)/shard_map/ppermute | solution.py:426
  97.8 4.9 %shard_map.104 = (s16[528,256]{1,0:T(8,128)(2,1)S(1)}, s16[528,256]{1,0:T(8,128)(2,1)S(1)}, s16[528,256]{1,0:T(8,128)(2,1)S(1)}, f32[16,128,256]{2,1,0:T(8,128)S...) custom-call(s32[30]{0:T(128)S(1)} %stack.121.meta, s32[8,128]{1,0:T(8,128)S(1)} %get-tuple-element.49.cols, ...), custom_call_target="tpu_custom_call" | custom-call | flops 1073741824 | bytes 65536 | tf_op jit(solution)/shard_map/pallas_call | solution.py:30
  109.2 3.0 %collective-permute-done.26.g3 = s16[528,256]{1,0:T(8,128)(2,1)S(1)} collective-permute-done((s16[528,256]{1,0:T(8,128)(2,1)S(1)}, s16[528,256]{1,0:T(8,128)(2,1)S(1)}, u32[]{:S(2)}, u32[]{:S(2)}) %collective-permute-start.26) | collective-permute-done | bytes 270368 | tf_op jit(solution)/shard_map/ppermute | solution.py:426
  118.5 4.4 %collective-permute-done.30.p2 = s16[528,256]{1,0:T(8,128)(2,1)S(1)} collective-permute-done((s16[528,256]{1,0:T(8,128)(2,1)S(1)}, s16[528,256]{1,0:T(8,128)(2,1)S(1)}, u32[]{:S(2)}, u32[]{:S(2)}) %collective-permute-start.30) | collective-permute-done | bytes 270368 | tf_op jit(solution)/shard_map/ppermute | solution.py:426
  122.9 2.8 %collective-permute-done.29.p3 = s16[528,256]{1,0:T(8,128)(2,1)S(1)} collective-permute-done((s16[528,256]{1,0:T(8,128)(2,1)S(1)}, s16[528,256]{1,0:T(8,128)(2,1)S(1)}, u32[]{:S(2)}, u32[]{:S(2)}) %collective-permute-start.29) | collective-permute-done | bytes 270368 | tf_op jit(solution)/shard_map/ppermute | solution.py:426
  132.4 4.9 %collective-permute-done.33.b3 = bf16[512,256]{1,0:T(8,128)(2,1)S(1)} collective-permute-done((bf16[512,256]{1,0:T(8,128)(2,1)S(1)}, bf16[512,256]{1,0:T(8,128)(2,1)S(1)}, u32[]{:S(2)}, u32[]{:S(2)}) %collective-permute-start.33) | collective-permute-done | bytes 262176 | tf_op jit(solution)/shard_map/ppermute | solution.py:426
  138.3 3.1 %shard_map.110 = bf16[512,256]{1,0:T(8,128)(2,1)S(1)} custom-call(s32[30]{0:T(128)S(1)} %stack.121.meta, s32[8,128]{1,0:T(8,128)S(1)} %get-tuple-element.49.cols, f32[128,128]{1,0:T(8,128)S(1)} %fusion.live, bf16[128,128,256]{2,1,0:T(8,128)(2,1)S(1)} %bitcast.53, bf16[128,128,256]{2,1,0:T(8,128)(2,1)S(1)} %bitcast.44, ...), custom_call_target="tpu_custom_call" | custom-call | flops 1073741824 | bytes 65536 | tf_op jit(solution)/shard_map/pallas_call | solution.py:30
  141.5 3.2 %shard_map.109 = (f32[512,256]{1,0:T(8,128)S(1)}, f32[512,256]{1,0:T(8,128)S(1)}, f32[8,128]{1,0:T(8,128)S(1)}) custom-call(s32[30]{0:T(128)S(1)} %stack.121.meta, s32[8,128]{1,0:T(8,128)S(1)} %get-tuple-element.49.cols, f32[128,128]{1,0:T(8,128)S(1)} %fusion.live, bf16[128,128,256]{2,1,0:T(8,128)(2,1)S(1)} %bitcast.54, bf16[128,128,256]{2,1,0:T(8,128)(2,1)S(1)} %bitcast.45, ...), custom_call_target="tpu_custom_call" | custom-call | flops 1073741824 | bytes 65536 | tf_op jit(solution)/shard_map/pallas_call | solution.py:30
  146.1 2.9 %collective-permute-start.37 = (bf16[128,256]{1,0:T(8,128)(2,1)S(1)}, bf16[128,256]{1,0:T(8,128)(2,1)S(1)}, u32[]{:S(2)}, u32[]{:S(2)}) collective-permute-start(bf16[128,256]{1,0:T(8,128)(2,1)S(1)} %get-tuple-element.89), channel_id=1, source_target_pairs={{0,4},{1,5},{2,6},{3,7},{4,0},{5,1},{6,2},{7,3},{8,12},{9,13},{10,... | collective-permute-start | bytes 196616 | tf_op jit(solution)/shard_map/ppermute | solution.py:426
  172.2 2.6 %collective-permute-done.46 = f32[24,128]{1,0:T(8,128)S(1)} collective-permute-done((f32[24,128]{1,0:T(8,128)S(1)}, f32[24,128]{1,0:T(8,128)S(1)}, u32[]{:S(2)}, u32[]{:S(2)}) %collective-permute-start.46) | collective-permute-done | bytes 12320 | tf_op jit(solution)/shard_map/ppermute | solution.py:426
  (133 shorter events, 93.8 us)
Async XLA Ops:
  3.6 7.1 %collective-permute-start.2 = (bf16[144,256]{1,0:T(8,128)(2,1)S(1)}, bf16[144,256]{1,0:T(8,128)(2,1)S(1)}, u32[]{:S(2)}, u32[]{:S(2)}) collective-permute-start(bf16[144,256]{1,0:T(8,128)(2,1)S(1)} %shard_map.94.a0), channel_id=1, source_target_pairs={{0,6},{1,7},{2,4},{3,5},{4,2},{5,3},{6,0},{7,1},{8,14},{9,15},{10,... | collective-permute-start | bytes 221192 | tf_op jit(solution)/shard_map/ppermute | solution.py:426
  6.8 6.6 %collective-permute-start.1 = (bf16[144,256]{1,0:T(8,128)(2,1)S(1)}, bf16[144,256]{1,0:T(8,128)(2,1)S(1)}, u32[]{:S(2)}, u32[]{:S(2)}) collective-permute-start(bf16[144,256]{1,0:T(8,128)(2,1)S(1)} %shard_map.94.a0), channel_id=1, source_target_pairs={{0,4},{1,5},{2,6},{3,7},{4,0},{5,1},{6,2},{7,3},{8,12},{9,13},{10,... | collective-permute-start | bytes 221192 | tf_op jit(solution)/shard_map/ppermute | solution.py:426
  13.4 23.5 %collective-permute-start.7 = (bf16[6,256,256]{2,1,0:T(8,128)(2,1)S(1)}, bf16[6,256,256]{2,1,0:T(8,128)(2,1)S(1)}, u32[]{:S(2)}, u32[]{:S(2)}) collective-permute-start(bf16[6,256,256]{2,1,0:T(8,128)(2,1)S(1)} %pad_maximum_fusion.t0), channel_id=1, source_target_pairs={{6,0},{14,8},{23,17},{31,25},{36,34},{44,42},{53,51},{61,59},{66,6... | collective-permute-start | bytes 2359304 | tf_op jit(solution)/shard_map/ppermute | solution.py:426
  14.7 22.2 %collective-permute-start.6 = (bf16[6,256,256]{2,1,0:T(8,128)(2,1)S(1)}, bf16[6,256,256]{2,1,0:T(8,128)(2,1)S(1)}, u32[]{:S(2)}, u32[]{:S(2)}) collective-permute-start(bf16[6,256,256]{2,1,0:T(8,128)(2,1)S(1)} %pad_maximum_fusion.t0), channel_id=1, source_target_pairs={{4,0},{12,8},{21,17},{29,25},{38,34},{46,42},{55,51},{63,59},{64,6... | collective-permute-start | bytes 2359304 | tf_op jit(solution)/shard_map/ppermute | solution.py:426
  16.0 20.9 %collective-permute-start.5 = (bf16[6,256,256]{2,1,0:T(8,128)(2,1)S(1)}, bf16[6,256,256]{2,1,0:T(8,128)(2,1)S(1)}, u32[]{:S(2)}, u32[]{:S(2)}) collective-permute-start(bf16[6,256,256]{2,1,0:T(8,128)(2,1)S(1)} %pad_maximum_fusion.t0), channel_id=1, source_target_pairs={{2,0},{10,8},{19,17},{27,25},{32,34},{40,42},{49,51},{57,59},{70,6... | collective-permute-start | bytes 2359304 | tf_op jit(solution)/shard_map/ppermute | solution.py:426
  38.9 6.5 %collective-permute-start.8 = (s16[528,256]{1,0:T(8,128)(2,1)S(1)}, s16[528,256]{1,0:T(8,128)(2,1)S(1)}, u32[]{:S(2)}, u32[]{:S(2)}) collective-permute-start(s16[528,256]{1,0:T(8,128)(2,1)S(1)} %get-tuple-element.54), channel_id=1, source_target_pairs={{0,32},{1,9},{2,34},{3,11},{4,36},{5,13},{6,38},{7,15},{8,40},{9,1... | collective-permute-start | bytes 811016 | tf_op jit(solution)/shard_map/ppermute | solution.py:426
  39.0 9.9 %collective-permute-start.9 = (s16[528,256]{1,0:T(8,128)(2,1)S(1)}, s16[528,256]{1,0:T(8,128)(2,1)S(1)}, u32[]{:S(2)}, u32[]{:S(2)}) collective-permute-start(s16[528,256]{1,0:T(8,128)(2,1)S(1)} %get-tuple-element.55), channel_id=1, source_target_pairs={{0,96},{1,25},{2,98},{3,27},{4,100},{5,29},{6,102},{7,31},{8,104},... | collective-permute-start | bytes 811016 | tf_op jit(solution)/shard_map/ppermute | solution.py:426
  42.0 8.0 %collective-permute-start.10 = (s16[528,256]{1,0:T(8,128)(2,1)S(1)}, s16[528,256]{1,0:T(8,128)(2,1)S(1)}, u32[]{:S(2)}, u32[]{:S(2)}) collective-permute-start(s16[528,256]{1,0:T(8,128)(2,1)S(1)} %get-tuple-element.56), channel_id=1, source_target_pairs={{0,64},{1,17},{2,66},{3,19},{4,68},{5,21},{6,70},{7,23},{8,72},{9,... | collective-permute-start | bytes 811016 | tf_op jit(solution)/shard_map/ppermute | solution.py:426
  51.2 8.1 %collective-permute-start.13 = (s16[528,256]{1,0:T(8,128)(2,1)S(1)}, s16[528,256]{1,0:T(8,128)(2,1)S(1)}, u32[]{:S(2)}, u32[]{:S(2)}) collective-permute-start(s16[528,256]{1,0:T(8,128)(2,1)S(1)} %get-tuple-element.58), channel_id=1, source_target_pairs={{0,16},{1,65},{2,18},{3,67},{4,20},{5,69},{6,22},{7,71},{8,24},{9,... | collective-permute-start | bytes 811016 | tf_op jit(solution)/shard_map/ppermute | solution.py:426
  51.8 10.2 %collective-permute-start.12 = (s16[528,256]{1,0:T(8,128)(2,1)S(1)}, s16[528,256]{1,0:T(8,128)(2,1)S(1)}, u32[]{:S(2)}, u32[]{:S(2)}) collective-permute-start(s16[528,256]{1,0:T(8,128)(2,1)S(1)} %get-tuple-element.58), channel_id=1, source_target_pairs={{0,24},{1,97},{2,26},{3,99},{4,28},{5,101},{6,30},{7,103},{8,16},{... | collective-permute-start | bytes 811016 | tf_op jit(solution)/shard_map/ppermute | solution.py:426
  55.8 6.5 %collective-permute-start.11 = (s16[528,256]{1,0:T(8,128)(2,1)S(1)}, s16[528,256]{1,0:T(8,128)(2,1)S(1)}, u32[]{:S(2)}, u32[]{:S(2)}) collective-permute-start(s16[528,256]{1,0:T(8,128)(2,1)S(1)} %get-tuple-element.58), channel_id=1, source_target_pairs={{0,8},{1,33},{2,10},{3,35},{4,12},{5,37},{6,14},{7,39},{8,0},{9,41... | collective-permute-start | bytes 811016 | tf_op jit(solution)/shard_map/ppermute | solution.py:426
  62.7 9.4 %collective-permute-start.16 = (bf16[512,256]{1,0:T(8,128)(2,1)S(1)}, bf16[512,256]{1,0:T(8,128)(2,1)S(1)}, u32[]{:S(2)}, u32[]{:S(2)}) collective-permute-start(bf16[512,256]{1,0:T(8,128)(2,1)S(1)} %get-tuple-element.60.a), channel_id=1, source_target_pairs={{0,96},{1,25},{2,98},{3,27},{4,100},{5,29},{6,102},{7,31},{8,104},... | collective-permute-start | bytes 786440 | tf_op jit(solution)/shard_map/ppermute | solution.py:426
  65.4 7.9 %collective-permute-start.15 = (bf16[512,256]{1,0:T(8,128)(2,1)S(1)}, bf16[512,256]{1,0:T(8,128)(2,1)S(1)}, u32[]{:S(2)}, u32[]{:S(2)}) collective-permute-start(bf16[512,256]{1,0:T(8,128)(2,1)S(1)} %get-tuple-element.60.a), channel_id=1, source_target_pairs={{0,64},{1,17},{2,66},{3,19},{4,68},{5,21},{6,70},{7,23},{8,72},{9,... | collective-permute-start | bytes 786440 | tf_op jit(solution)/shard_map/ppermute | solution.py:426
  65.4 8.7 %collective-permute-start.14 = (bf16[512,256]{1,0:T(8,128)(2,1)S(1)}, bf16[512,256]{1,0:T(8,128)(2,1)S(1)}, u32[]{:S(2)}, u32[]{:S(2)}) collective-permute-start(bf16[512,256]{1,0:T(8,128)(2,1)S(1)} %get-tuple-element.60.a), channel_id=1, source_target_pairs={{0,32},{1,9},{2,34},{3,11},{4,36},{5,13},{6,38},{7,15},{8,40},{9,1... | collective-permute-start | bytes 786440 | tf_op jit(solution)/shard_map/ppermute | solution.py:426
  102.7 6.5 %collective-permute-start.25 = (s16[528,256]{1,0:T(8,128)(2,1)S(1)}, s16[528,256]{1,0:T(8,128)(2,1)S(1)}, u32[]{:S(2)}, u32[]{:S(2)}) collective-permute-start(s16[528,256]{1,0:T(8,128)(2,1)S(1)} %get-tuple-element.72), channel_id=1, source_target_pairs={{0,32},{1,9},{2,34},{3,11},{4,36},{5,13},{6,38},{7,15},{8,40},{9,1... | collective-permute-start | bytes 811016 | tf_op jit(solution)/shard_map/ppermute | solution.py:426
  103.3 9.0 %collective-permute-start.26 = (s16[528,256]{1,0:T(8,128)(2,1)S(1)}, s16[528,256]{1,0:T(8,128)(2,1)S(1)}, u32[]{:S(2)}, u32[]{:S(2)}) collective-permute-start(s16[528,256]{1,0:T(8,128)(2,1)S(1)} %get-tuple-element.73), channel_id=1, source_target_pairs={{0,96},{1,25},{2,98},{3,27},{4,100},{5,29},{6,102},{7,31},{8,104},... | collective-permute-start | bytes 811016 | tf_op jit(solution)/shard_map/ppermute | solution.py:426
  105.4 8.7 %collective-permute-start.27 = (s16[528,256]{1,0:T(8,128)(2,1)S(1)}, s16[528,256]{1,0:T(8,128)(2,1)S(1)}, u32[]{:S(2)}, u32[]{:S(2)}) collective-permute-start(s16[528,256]{1,0:T(8,128)(2,1)S(1)} %get-tuple-element.74), channel_id=1, source_target_pairs={{0,64},{1,17},{2,66},{3,19},{4,68},{5,21},{6,70},{7,23},{8,72},{9,... | collective-permute-start | bytes 811016 | tf_op jit(solution)/shard_map/ppermute | solution.py:426
  114.7 8.1 %collective-permute-start.30 = (s16[528,256]{1,0:T(8,128)(2,1)S(1)}, s16[528,256]{1,0:T(8,128)(2,1)S(1)}, u32[]{:S(2)}, u32[]{:S(2)}) collective-permute-start(s16[528,256]{1,0:T(8,128)(2,1)S(1)} %get-tuple-element.77), channel_id=1, source_target_pairs={{0,16},{1,65},{2,18},{3,67},{4,20},{5,69},{6,22},{7,71},{8,24},{9,... | collective-permute-start | bytes 811016 | tf_op jit(solution)/shard_map/ppermute | solution.py:426
  116.5 9.2 %collective-permute-start.29 = (s16[528,256]{1,0:T(8,128)(2,1)S(1)}, s16[528,256]{1,0:T(8,128)(2,1)S(1)}, u32[]{:S(2)}, u32[]{:S(2)}) collective-permute-start(s16[528,256]{1,0:T(8,128)(2,1)S(1)} %get-tuple-element.77), channel_id=1, source_target_pairs={{0,24},{1,97},{2,26},{3,99},{4,28},{5,101},{6,30},{7,103},{8,16},{... | collective-permute-start | bytes 811016 | tf_op jit(solution)/shard_map/ppermute | solution.py:426
  118.5 7.2 %collective-permute-start.28 = (s16[528,256]{1,0:T(8,128)(2,1)S(1)}, s16[528,256]{1,0:T(8,128)(2,1)S(1)}, u32[]{:S(2)}, u32[]{:S(2)}) collective-permute-start(s16[528,256]{1,0:T(8,128)(2,1)S(1)} %get-tuple-element.77), channel_id=1, source_target_pairs={{0,8},{1,33},{2,10},{3,35},{4,12},{5,37},{6,14},{7,39},{8,0},{9,41... | collective-permute-start | bytes 811016 | tf_op jit(solution)/shard_map/ppermute | solution.py:426
  126.9 10.5 %collective-permute-start.33 = (bf16[512,256]{1,0:T(8,128)(2,1)S(1)}, bf16[512,256]{1,0:T(8,128)(2,1)S(1)}, u32[]{:S(2)}, u32[]{:S(2)}) collective-permute-start(bf16[512,256]{1,0:T(8,128)(2,1)S(1)} %get-tuple-element.80.a), channel_id=1, source_target_pairs={{0,96},{1,25},{2,98},{3,27},{4,100},{5,29},{6,102},{7,31},{8,104},... | collective-permute-start | bytes 786440 | tf_op jit(solution)/shard_map/ppermute | solution.py:426
  128.8 8.5 %collective-permute-start.32 = (bf16[512,256]{1,0:T(8,128)(2,1)S(1)}, bf16[512,256]{1,0:T(8,128)(2,1)S(1)}, u32[]{:S(2)}, u32[]{:S(2)}) collective-permute-start(bf16[512,256]{1,0:T(8,128)(2,1)S(1)} %get-tuple-element.80.a), channel_id=1, source_target_pairs={{0,64},{1,17},{2,66},{3,19},{4,68},{5,21},{6,70},{7,23},{8,72},{9,... | collective-permute-start | bytes 786440 | tf_op jit(solution)/shard_map/ppermute | solution.py:426
  129.6 8.6 %collective-permute-start.31 = (bf16[512,256]{1,0:T(8,128)(2,1)S(1)}, bf16[512,256]{1,0:T(8,128)(2,1)S(1)}, u32[]{:S(2)}, u32[]{:S(2)}) collective-permute-start(bf16[512,256]{1,0:T(8,128)(2,1)S(1)} %get-tuple-element.80.a), channel_id=1, source_target_pairs={{0,32},{1,9},{2,34},{3,11},{4,36},{5,13},{6,38},{7,15},{8,40},{9,1... | collective-permute-start | bytes 786440 | tf_op jit(solution)/shard_map/ppermute | solution.py:426
  144.9 6.5 %collective-permute-start.36 = (bf16[128,256]{1,0:T(8,128)(2,1)S(1)}, bf16[128,256]{1,0:T(8,128)(2,1)S(1)}, u32[]{:S(2)}, u32[]{:S(2)}) collective-permute-start(bf16[128,256]{1,0:T(8,128)(2,1)S(1)} %get-tuple-element.88), channel_id=1, source_target_pairs={{0,6},{1,7},{2,4},{3,5},{4,2},{5,3},{6,0},{7,1},{8,14},{9,15},{10,... | collective-permute-start | bytes 196616 | tf_op jit(solution)/shard_map/ppermute | solution.py:426
  (38 other events, 286.1 us)
